TPU v7x, 32 devices: a whole 2x2x4 slice. The times are simulated.
32 devices in a mesh: groups: 2 (over y), tensor: 4 (over z), sub: 4 (over x, core).
Axes of the slice: x: 2, y: 2, z: 4, core: 2. Of those that a mesh axis runs over, the one named last changes fastest.
Arguments:
- tokens: bfloat16 [256, 8192], P(('groups', 'tensor'), 'sub'), parts along dimension 0, may hold values from -6 to 6
- request_adapter_ids: int32 [2], P('groups'), parts along dimension 0, may hold values from 0 to 11
- slot_of_adapter: int32 [24], P('groups'), parts along dimension 0, may hold values from 0 to 11, each once
- gate_weight: bfloat16 [8192, 14336], P('sub', 'tensor'), may hold values from -0.0625 to 0.0625
- up_weight: bfloat16 [8192, 14336], P('sub', 'tensor'), may hold values from -0.0625 to 0.0625
- down_weight: bfloat16 [14336, 8192], P('tensor', 'sub'), may hold values from -0.046875 to 0.046875
- adapter_input_maps: bfloat16 [24, 8192, 128], P(('groups', 'tensor'), 'sub'), parts along dimension 0, may hold values from -0.0625 to 0.0625
- adapter_output_maps: bfloat16 [24, 2, 64, 14336], P(('groups', 'tensor'), None, 'sub'), parts along dimension 0, may hold values from -0.75 to 0.75
Outputs:
- layer_out: bfloat16 [256, 8192], P(('groups', 'tensor'), 'sub'), parts along dimension 0
There are 2 independent parts, one for each index of `groups`. A program takes and returns all parts, laid end to end along the dimension named above; an argument that names none is the same for every part. Nothing has to cross between parts.
Inputs may be any that keep to these rules, and one draw needn't show every extreme that they name: `slot_of_adapter`: a permutation: every storage slot appears exactly once; slot k is stored at tensor index k // 3. `request_adapter_ids`: several requests may name the same adapter.
All inputs are finite; a program needn't handle non-finite values.
Results may differ from a plain program's by a relative error of at most 0.018.
Values may be sent and summed in bfloat16 or wider, within the bound.
A program may use at most 192 MiB of HBM per device.

v0:
```python
import jax
import jax.numpy as jnp
from jax import lax
from jax.sharding import PartitionSpec as P


def shards(
    tokens,
    request_adapter_ids,
    slot_of_adapter,
    gate_weight,
    up_weight,
    down_weight,
    adapter_input_maps,
    adapter_output_maps,
):
    my_owner = lax.axis_index("tensor")
    sub_index = lax.axis_index("sub")
    requests = request_adapter_ids.shape[0]
    kept_slot_list = adapter_input_maps.shape[0]
    rank_columns_block = adapter_output_maps.shape[2]
    combined_rank = adapter_input_maps.shape[2] // 2
    collected_rows = lax.all_gather(tokens, "tensor", axis=0, tiled=True)
    overall_row_count = collected_rows.shape[0]
    block_rows = overall_row_count // requests
    feat_cols = collected_rows.shape[1]
    slot_count = slot_of_adapter.shape[0]
    matches = request_adapter_ids[:, None] == jnp.arange(slot_count, dtype=jnp.int32)[None, :]
    picked = jnp.sum(jnp.where(matches, slot_of_adapter[None, :], 0), axis=1)
    owners = picked // kept_slot_list
    local_index = picked % kept_slot_list
    local_match = local_index[:, None] == jnp.arange(kept_slot_list, dtype=jnp.int32)[None, :]
    local_selection = ((owners == my_owner)[:, None] & local_match).astype(jnp.bfloat16)
    down_weight_panel = jnp.einsum(
        "ny,yle->nle", local_selection, adapter_input_maps, preferred_element_type=jnp.float32
    ).astype(jnp.bfloat16)
    grouped = collected_rows.reshape(requests, block_rows, feat_cols)
    reduced_piece = jnp.einsum(
        "qcd,qdk->qck", grouped, down_weight_panel, preferred_element_type=jnp.float32
    )
    shrink = lax.psum(
        reduced_piece.reshape(overall_row_count, 2 * combined_rank), ("tensor", "sub")
    ).astype(jnp.bfloat16)
    my_shrink = lax.dynamic_slice_in_dim(
        shrink.reshape(requests, block_rows, 2, combined_rank),
        sub_index * rank_columns_block,
        rank_columns_block,
        3,
    )
    outgoing = jnp.einsum(
        "np,pmls->nmls", local_selection, adapter_output_maps, preferred_element_type=jnp.float32
    ).astype(jnp.bfloat16)
    arrived = lax.all_to_all(outgoing[None], "tensor", split_axis=4, concat_axis=0, tiled=True)
    up_weight_panel = jnp.sum(arrived, axis=0)
    adapter_correction = jnp.einsum(
        "gtoz,gozy->gtoy", my_shrink, up_weight_panel, preferred_element_type=jnp.float32
    )
    adapter_correction = adapter_correction.reshape(overall_row_count, 2, up_weight_panel.shape[3])
    gate_output_piece = (
        jnp.dot(collected_rows, gate_weight, preferred_element_type=jnp.float32)
        + adapter_correction[:, 0]
    )
    up_output_piece = (
        jnp.dot(collected_rows, up_weight, preferred_element_type=jnp.float32)
        + adapter_correction[:, 1]
    )
    gate_sum, up_sum = (
        lax.psum_scatter(
            gate_output_piece.astype(jnp.bfloat16), "sub", scatter_dimension=1, tiled=True
        ).astype(jnp.float32),
        lax.psum_scatter(
            up_output_piece.astype(jnp.bfloat16), "sub", scatter_dimension=1, tiled=True
        ).astype(jnp.float32),
    )
    hidden = (jax.nn.silu(gate_sum) * up_sum).astype(jnp.bfloat16)
    hidden = lax.all_gather(hidden, "sub", axis=1, tiled=True)
    down_sum = lax.psum_scatter(
        jnp.dot(hidden, down_weight, preferred_element_type=jnp.float32).astype(jnp.bfloat16),
        "tensor",
        scatter_dimension=0,
        tiled=True,
    ).astype(jnp.float32)
    return (tokens.astype(jnp.float32) + down_sum).astype(jnp.bfloat16)


def solution(mesh):
    in_specs = (
        P(("groups", "tensor"), "sub"),
        P("groups"),
        P("groups"),
        P("sub", "tensor"),
        P("sub", "tensor"),
        P("tensor", "sub"),
        P(("groups", "tensor"), "sub", None),
        P(("groups", "tensor"), None, "sub", None),
    )
    out_specs = P(("groups", "tensor"), "sub")
    return jax.shard_map(shards, mesh=mesh, in_specs=in_specs, out_specs=out_specs, check_vma=False)
```

profile of v0, /device:TPU:1, one launch (start us, length us, event | category | flops | bytes accessed | tf_op | source)
XLA Modules:
  0.0 275.2 jit_solution(10567861146368764088)
XLA Ops:
  7.3 1.3 fusion.18
  10.4 5.2 %fusion.3 = bf16[1,2,16,14336]{3,0,2,1:T(2,128)(2,1)} fusion(bf16[3,2,16,14336]{3,2,1,0:T(8,128)(2,1)S(1)} %copy-done, pred[]{:T(512)} %bitcast.5, s32[]{:T(128)} %bitcast.6), kind=kOutput, calls=%fused_computation.7 | convolution fusion | flops 2752518 | bytes 3670021 | tf_op jit(solution)/shard_map/np,pmls->nmls/dot_general | solution.py:50
  15.6 18.0 %copy.15 = bf16[1,2,16,14336]{2,1,3,0:T(2,128)(2,1)} copy(bf16[1,2,16,14336]{3,0,2,1:T(2,128)(2,1)} %fusion.3) | data formatting | bytes 1835008 | tf_op jit(solution)/shard_map/np,pmls->nmls/dot_general | solution.py:50
  33.6 7.2 %fusion.20 = bf16[14336,1,1,2,16]{4,3,2,1,0:T(2,128)(2,1)} fusion(bf16[1,2,16,14336]{2,1,3,0:T(2,128)(2,1)} %copy.15), kind=kLoop, calls=%fused_computation.33 | loop fusion | bytes 1835008
  40.8 9.8 %reshape.65 = bf16[4,2,57344]{2,1,0:T(2,128)(2,1)} reshape(bf16[14336,1,1,2,16]{4,3,2,1,0:T(2,128)(2,1)} %fusion.20) | data formatting | bytes 1835008
  50.6 5.4 %all-to-all-start = ((bf16[4,2,57344]{2,1,0:T(2,128)(2,1)}), bf16[4,2,57344]{2,1,0:T(2,128)(2,1)S(1)}, u32[]{:S(2)}, u32[]{:S(2)}) async-start(bf16[4,2,57344]{2,1,0:T(2,128)(2,1)} %reshape.65), calls=%async_computation | async-start | bytes 1835008 | tf_op jit(solution)/shard_map/all_to_all | solution.py:53
  56.0 30.2 %all_gather.6 = bf16[128,2048]{1,0:T(8,128)(2,1)S(1)} all-gather(bf16[32,2048]{1,0:T(8,128)(2,1)S(1)} %copy-done.3), channel_id=1, replica_groups=mesh['groups'=2,'tensor'=4,'sub'=4] {'tensor'}, dimensions={0}, use_global_device_ids=true | all-gather | bytes 655360 | tf_op jit(solution)/shard_map/all_gather | solution.py:23
  86.2 2.9 %fusion.5 = f32[1,2048,128]{2,0,1:T(1,128)S(1)} fusion(bf16[3,2048,128]{2,1,0:T(8,128)(2,1)} %param.14, pred[]{:T(512)} %bitcast.5, s32[]{:T(128)} %bitcast.6), kind=kOutput, calls=%fused_computation.10 | convolution fusion | flops 1572870 | bytes 2621445 | tf_op jit(solution)/shard_map/ny,yle->nle/dot_general | solution.py:34
  89.4 56.5 %psum.7 = bf16[128,128]{0,1:T(8,128)(2,1)S(1)} all-reduce(f32[128,128]{0,1:T(8,128)S(1)} %convolution_bitcast_fusion.1), channel_id=1, replica_groups=mesh['groups'=2,'tensor'=4,'sub'=4] {'tensor','sub'}, use_global_device_ids=true, to_apply=%region_2.3 | all-reduce | flops 16384 | bytes 98304 | tf_op jit(solution)/shard_map/psum | solution.py:41
  145.9 6.4 %reshape.66 = bf16[14336,1,1,2,16]{4,3,2,1,0:T(2,128)(2,1)} reshape(bf16[4,2,57344]{2,1,0:T(2,128)(2,1)S(1)} %all-to-all-done) | data formatting | bytes 1835008
  152.2 12.0 %reduce_sum.22 = bf16[2,16,3584]{1,0,2:T(2,128)(2,1)S(1)} reduce(bf16[2,16,4,3584]{1,0,3,2:T(2,128)(2,1)} %bitcast.63, bf16[]{:T(256)} %constant.43.clone.1), dimensions={2}, to_apply=%region_1.2 | reduce | flops 344064 | bytes 1146882 | tf_op jit(solution)/shard_map/reduce_sum | solution.py:54
  164.9 1.8 copy-done.2
  166.7 7.3 %fusion.2 = bf16[128,3584]{1,0:T(8,128)(2,1)S(1)} fusion(bf16[128,2048]{1,0:T(8,128)(2,1)S(1)} %all_gather.6, bf16[2048,3584]{1,0:T(8,128)(2,1)} %param.12, f32[128,2,3584]{2,0,1:T(8,128)S(1)} %convolution_bitcast_fusion), kind=kOutput, calls=%fused_computation.6 | convolution fusion | flops 1879965696 | bytes 17956864 | tf_op jit(solution)/shard_map/dot_general | solution.py:64
  174.0 1.3 copy.21
  175.4 7.8 %fusion.1 = bf16[128,3584]{1,0:T(8,128)(2,1)S(1)} fusion(bf16[128,2048]{1,0:T(8,128)(2,1)S(1)} %all_gather.6, bf16[2048,3584]{1,0:T(8,128)(2,1)} %param.11, f32[128,2,3584]{2,0,1:T(8,128)} %copy-done.2), kind=kOutput, calls=%fused_computation.5 | convolution fusion | flops 1879965696 | bytes 17956864 | tf_op jit(solution)/shard_map/dot_general | solution.py:60
  183.1 1.3 copy.19
  184.5 16.7 %reduce-scatter.12.cloned.1.call-done = bf16[896,128]{1,0:T(8,128)(2,1)} async-done(((bf16[3584,128]{1,0:T(8,128)(2,1)}), bf16[896,128]{1,0:T(8,128)(2,1)}) %reduce-scatter.12.cloned.1.call-update) | async-done | bytes 229392
  201.2 1.1 copy.22
  202.3 25.7 %reduce-scatter.10.cloned.1.call-done = bf16[896,128]{1,0:T(8,128)(2,1)} async-done(((bf16[3584,128]{1,0:T(8,128)(2,1)}), bf16[896,128]{1,0:T(8,128)(2,1)}) %reduce-scatter.10.cloned.1.call-update) | async-done | bytes 229392
  228.0 1.1 copy.20
  229.2 9.4 %all_gather.7 = bf16[128,3584]{1,0:T(8,128)(2,1)S(1)} all-gather(bf16[128,896]{1,0:T(8,128)(2,1)S(1)} %fusion.13), channel_id=1, replica_groups=mesh['groups'=2,'tensor'=4,'sub'=4] {'sub'}, dimensions={1}, use_global_device_ids=true | all-gather | bytes 1146880 | tf_op jit(solution)/shard_map/all_gather | solution.py:76
  238.7 8.5 %convolution_convert_fusion = bf16[128,2048]{1,0:T(8,128)(2,1)} fusion(bf16[128,3584]{1,0:T(8,128)(2,1)S(1)} %all_gather.7, bf16[3584,2048]{1,0:T(8,128)(2,1)} %param.13), kind=kOutput, calls=%fused_computation.9 | convolution fusion | flops 1879310336 | bytes 16121856 | tf_op jit(solution)/shard_map/dot_general | solution.py:78
  247.2 19.9 %reduce-scatter.8.cloned.1.call-done = bf16[32,2048]{1,0:T(8,128)(2,1)} async-done(((bf16[128,2048]{1,0:T(8,128)(2,1)}), bf16[32,2048]{1,0:T(8,128)(2,1)}) %reduce-scatter.8.cloned.1.call-update) | async-done | bytes 131088 | tf_op jit(solution)/shard_map/reduce_scatter | solution.py:77
  267.1 1.6 add_convert_fusion
  (17 shorter events, 1.3 us)
Async XLA Ops:
  6.5 3.8 %copy-start = (bf16[3,2,16,14336]{3,2,1,0:T(8,128)(2,1)S(1)}, bf16[3,2,16,14336]{3,2,1,0:T(8,128)(2,1)}, u32[]{:S(2)}) copy-start(bf16[3,2,16,14336]{3,2,1,0:T(8,128)(2,1)} %param.15) | copy-start | bytes 8257540
  40.8 15.2 %copy-start.3 = (bf16[32,2048]{1,0:T(8,128)(2,1)S(1)}, bf16[32,2048]{1,0:T(8,128)(2,1)}, u32[]{:S(2)}) copy-start(bf16[32,2048]{1,0:T(8,128)(2,1)} %param.8) | copy-start | bytes 393220
  50.6 95.3 %all-to-all-start = ((bf16[4,2,57344]{2,1,0:T(2,128)(2,1)}), bf16[4,2,57344]{2,1,0:T(2,128)(2,1)S(1)}, u32[]{:S(2)}, u32[]{:S(2)}) async-start(bf16[4,2,57344]{2,1,0:T(2,128)(2,1)} %reshape.65), calls=%async_computation | async-start | bytes 1835008 | tf_op jit(solution)/shard_map/all_to_all | solution.py:53
  56.0 145.2 %reduce-scatter.12.cloned.1.call-start = ((), (), s32[]{:S(2)}) async-start(), calls=%async_computation.6 | async-start | bytes 1146880
  164.9 1.8 copy-start.2
  175.3 52.7 %reduce-scatter.10.cloned.1.call-start = ((), (), s32[]{:S(2)}) async-start(), calls=%async_computation.5 | async-start | bytes 1146880
  184.4 82.7 %reduce-scatter.8.cloned.1.call-start = ((), (), s32[]{:S(2)}) async-start(), calls=%async_computation.4 | async-start | bytes 655360 | tf_op jit(solution)/shard_map/reduce_scatter | solution.py:77
  238.7 30.0 %copy-start.1 = (bf16[3,2,16,14336]{3,2,1,0:T(8,128)(2,1)S(1)}, bf16[3,2,16,14336]{3,2,1,0:T(8,128)(2,1)}, u32[]{:S(2)}) copy-start(bf16[3,2,16,14336]{3,2,1,0:T(8,128)(2,1)} %param.15) | copy-start | bytes 8257540
Sparse Core Ops, SparseCore 0:
  175.4 25.7 reduce-scatter.11
  203.9 24.0 reduce-scatter.9
  247.3 19.7 reduce-scatter.7
where the time goes:
time: 279 us; the launch traced here: 275 us
  blocking collectives  96.1 us (34%)
  waiting for transfers between devices  62.4 us (22%)
  local copies, waits for them, and re-layouts  47.9 us (17%)
  matrix products  32.6 us (12%)
  between operations  15.7 us (6%)
  other arithmetic  15 us (5%)
  starting transfers between devices  5.51 us (2%)
    psum x1, blocking collectives, shards(): lax.psum(reduced_piece.reshape(overall_row_count, 2 * combined_rank), ('t...  56.5 us
    unnamed x5, waiting for transfers between devices  42.5 us
    all_gather x1, blocking collectives, shards(): collected_rows = lax.all_gather(tokens, 'tensor', axis=0, tiled=True)  30.2 us
    unnamed x15, local copies, waits for them, and re-layouts  29.9 us
    reduce_scatter x1, waiting for transfers between devices, shards(): lax.psum_scatter(jnp.dot(hidden, down_weight, preferred_element_type=jnp....  19.9 us
    dot_general x1, local copies, waits for them, and re-layouts, shards(): jnp.einsum('np,pmls->nmls', local_selection, adapter_output_maps, preferr...  18 us
    reduce_sum x1, other arithmetic, shards(): up_weight_panel = jnp.sum(arrived, axis=0)  12 us
    all_gather x1, blocking collectives, shards(): hidden = lax.all_gather(hidden, 'sub', axis=1, tiled=True)  9.43 us
  transfers between devices with their start and end apart: 4, of which 3 were waited for; matrix products, arithmetic and copies ran while one was open for 5% of the time, Pallas kernels for 0%

commit v1 on v0

v1 whole, which is shorter than its diff:
```python
import functools

import jax
import jax.numpy as jnp
from jax import lax
from jax.experimental import pallas as pl
from jax.experimental.pallas import tpu as pltpu
from jax.sharding import PartitionSpec as P

MESH = pl.DeviceIdType.MESH
F32 = jnp.float32
BF16 = jnp.bfloat16


def tile_of(width, choices):
    for choice in choices:
        if width % choice == 0:
            return choice
    return width


def aligned(index, size):
    return pl.ds(pl.multiple_of(index * size, size), size)


def block_kernel(
    cfg,
    ids_ref,
    slots_ref,
    tok_hbm,
    gate_hbm,
    up_hbm,
    down_hbm,
    imap_hbm,
    omap_hbm,
    out_ref,
    x_buf,
    w_buf,
    d_buf,
    imap,
    omap,
    b_send,
    b_recv,
    sh1_send,
    sh1_recv,
    sh2_send,
    sh2_recv,
    s_cols,
    acc,
    part,
    p_recv,
    x_send,
    x_recv,
    hid,
    d_part,
    d_recv,
    load_sem,
    w_sem,
    dw_sem,
    tok_s,
    tok_r,
    b_s,
    b_r,
    sh1_s,
    sh1_r,
    sh2_s,
    sh2_r,
    p_s,
    p_r,
    x_s,
    x_r,
    h_s,
    h_r,
    f_s,
    f_r,
    d_s,
    d_r,
):
    nt, ns, nreq, kept, rb, rank = cfg["nt"], cfg["ns"], cfg["req"], cfg["kept"], cfg["rb"], cfg["rank"]
    rows, hcols, dcols = cfg["rows"], cfg["hcols"], cfg["dcols"]
    tn, tw, dn, dw = cfg["tn"], cfg["tw"], cfg["dn"], cfg["dw"]
    nc, nd, lead = hcols // tn, dcols // dn, cfg["lead"]
    rpt, rps, blk, npair = rows // nt, rows // ns, rows // nreq, ns // 2
    rr = 2 * rb
    t = lax.axis_index("tensor")
    s = lax.axis_index("sub")
    pair, core = lax.div(s, 2), lax.rem(s, 2)
    mate = pair * 2 + (1 - core)
    t_peers = [lax.rem(t + i, nt) for i in range(1, nt)]
    s_peers = [lax.rem(s + i, ns) for i in range(1, ns)]
    j_peers = [lax.rem(pair + i, npair) for i in range(1, npair)]

    def remote(src, dst, ssem, rsem, dev):
        return pltpu.make_async_remote_copy(
            src_ref=src, dst_ref=dst, send_sem=ssem, recv_sem=rsem, device_id=dev, device_id_type=MESH
        )

    sent = []

    def send(*args):
        copy = remote(*args)
        copy.start()
        sent.append(copy)

    l_omap = pltpu.make_async_copy(omap_hbm, omap, load_sem.at[0])
    l_tok = pltpu.make_async_copy(tok_hbm, x_buf.at[aligned(t, rpt), :], load_sem.at[1])
    l_imap = pltpu.make_async_copy(imap_hbm, imap, load_sem.at[2])
    l_omap.start()
    l_tok.start()
    l_imap.start()
    l_w = []
    for k in range(nc):
        cols = pl.ds(k * tn, tn)
        pair_loads = [
            pltpu.make_async_copy(src.at[:, cols], w_buf.at[g, :, cols], w_sem.at[g, k])
            for g, src in enumerate((gate_hbm, up_hbm))
        ]
        for copy in pair_loads:
            copy.start()
        l_w.append(pair_loads)

    barrier = pltpu.get_barrier_semaphore()
    for p in t_peers:
        pl.semaphore_signal(barrier, inc=1, device_id={"tensor": p}, device_id_type=MESH)
    for p in s_peers:
        pl.semaphore_signal(barrier, inc=1, device_id={"sub": p}, device_id_type=MESH)
    pl.semaphore_wait(barrier, nt + ns - 2)

    for i, p in enumerate(t_peers):
        send(tok_hbm, x_buf.at[aligned(t, rpt), :], tok_s.at[i], tok_r.at[t], {"tensor": p})

    slots = [slots_ref[ids_ref[q]] for q in range(nreq)]
    local = [lax.rem(v, kept) for v in slots]
    mine = [jnp.where(lax.div(v, kept) == t, 1.0, 0.0).astype(F32) for v in slots]

    l_omap.wait()
    for q in range(nreq):
        for c in range(nt):
            theirs = omap[local[q], :, c * hcols : (c + 1) * hcols]
            b_send[c, q * rr : (q + 1) * rr, :] = (theirs.astype(F32) * mine[q]).astype(BF16)
    for k in range(nc):
        cols = pl.ds(k * tn, tn)
        for i, p in enumerate(t_peers):
            send(
                b_send.at[p, :, cols],
                b_recv.at[t, :, cols],
                b_s.at[i, k],
                b_r.at[t, k],
                {"tensor": p},
            )

    l_imap.wait()
    l_tok.wait()
    for p in t_peers:
        remote(tok_hbm, x_buf.at[aligned(p, rpt), :], tok_s.at[0], tok_r.at[p], {"tensor": p}).wait_recv()

    for q in range(nreq):
        span = slice(q * blk, (q + 1) * blk)
        piece = jnp.dot(x_buf[span, :], imap[local[q]], preferred_element_type=F32) * mine[q]
        flipped = piece.T
        for d in range(ns):
            sh1_send[d, 0:rb, span] = flipped[d * rb : (d + 1) * rb]
            sh1_send[d, rb:rr, span] = flipped[rank + d * rb : rank + (d + 1) * rb]
    for i, p in enumerate(s_peers):
        send(sh1_send.at[p], sh1_recv.at[s], sh1_s.at[i], sh1_r.at[s], {"sub": p})

    l_d = []
    for n in range(nd):
        cols = pl.ds(n * dn, dn)
        copy = pltpu.make_async_copy(down_hbm.at[:, cols], d_buf.at[:, cols], dw_sem.at[n])
        copy.start()
        l_d.append(copy)

    per = tn // tw

    def matmul(k):
        for copy in l_w[k]:
            copy.wait()

        def body(j, carry):
            g, c = lax.div(j, per), lax.rem(j, per)
            if per == 1:
                into, cols = pl.ds(0, tw), pl.ds(k * tn, tw)
            else:
                into, cols = aligned(c, tw), pl.ds(pl.multiple_of(k * tn + c * tw, 128), tw)
            acc[k % lead, g, :, into] = jnp.dot(x_buf[...], w_buf[g, :, cols], preferred_element_type=F32)
            return carry

        lax.fori_loop(0, 2 * per, body, 0)

    def finish(k):
        cols = pl.ds(k * tn, tn)
        for p in t_peers:
            remote(
                b_send.at[p, :, cols], b_recv.at[p, :, cols], b_s.at[0, k], b_r.at[p, k], {"tensor": p}
            ).wait_recv()
        total = b_send[t, :, cols].astype(F32)
        for p in t_peers:
            total += b_recv[p, :, cols].astype(F32)
        maps = total.astype(BF16)
        for g in range(2):
            for q in range(nreq):
                span = slice(q * blk, (q + 1) * blk)
                part[g, span, cols] = (
                    acc[k % lead, g, span, :]
                    + jnp.dot(s_cols[g, span, :], maps[q * rr : (q + 1) * rr], preferred_element_type=F32)
                ).astype(BF16)
        for j in j_peers + [pair]:
            send(
                part.at[:, aligned(2 * j + 1 - core, rps), cols],
                p_recv.at[j, :, :, cols],
                p_s.at[j, k],
                p_r.at[j, k],
                {"sub": mate},
            )

    def wait_mate(j, k):
        cols = pl.ds(k * tn, tn)
        remote(
            part.at[:, aligned(2 * j + 1 - core, rps), cols],
            p_recv.at[j, :, :, cols],
            p_s.at[j, k],
            p_r.at[j, k],
            {"sub": mate},
        ).wait_recv()

    def across(k):
        cols = pl.ds(k * tn, tn)
        for j in j_peers:
            wait_mate(j, k)
            x_send[j, :, :, cols] = (
                part[:, aligned(2 * j + core, rps), cols].astype(F32) + p_recv[j, :, :, cols].astype(F32)
            ).astype(BF16)
            send(
                x_send.at[j, :, :, cols],
                x_recv.at[pair, :, :, cols],
                x_s.at[j, k],
                x_r.at[pair, k],
                {"sub": 2 * j + core},
            )

    def activate(k):
        cols = pl.ds(k * tn, tn)
        wait_mate(pair, k)
        total = part[:, aligned(s, rps), cols].astype(F32) + p_recv[pair, :, :, cols].astype(F32)
        for j in j_peers:
            remote(
                x_send.at[j, :, :, cols],
                x_recv.at[j, :, :, cols],
                x_s.at[j, k],
                x_r.at[j, k],
                {"sub": 2 * j + core},
            ).wait_recv()
            total += x_recv[j, :, :, cols].astype(F32)
        gate, up = total[0], total[1]
        mine_rows = hid.at[aligned(s, rps), cols]
        hid[aligned(s, rps), cols] = (gate / (1.0 + jnp.exp(-gate)) * up).astype(BF16)
        for j in j_peers:
            send(mine_rows, mine_rows, h_s.at[j, k], h_r.at[pair, k], {"sub": 2 * j + core})
        send(mine_rows, mine_rows, f_s.at[pair, k], f_r.at[pair, k], {"sub": mate})

    def relay(k):
        cols = pl.ds(k * tn, tn)
        for j in j_peers:
            theirs = hid.at[aligned(2 * j + core, rps), cols]
            remote(theirs, theirs, h_s.at[j, k], h_r.at[j, k], {"sub": 2 * j + core}).wait_recv()
            send(theirs, theirs, f_s.at[j, k], f_r.at[j, k], {"sub": mate})

    matmul(0)

    mine_sum = sh1_send[s]
    for p in s_peers:
        remote(sh1_send.at[p], sh1_recv.at[p], sh1_s.at[0], sh1_r.at[p], {"sub": p}).wait_recv()
        mine_sum += sh1_recv[p]
    sh2_send[...] = mine_sum.astype(BF16)
    for i, p in enumerate(t_peers):
        send(sh2_send, sh2_recv.at[t], sh2_s.at[i], sh2_r.at[t], {"tensor": p})

    for k in range(1, lead):
        matmul(k)

    shrink = sh2_send[...].astype(F32)
    for p in t_peers:
        remote(sh2_send, sh2_recv.at[p], sh2_s.at[0], sh2_r.at[p], {"tensor": p}).wait_recv()
        shrink += sh2_recv[p].astype(F32)
    is_gate = lax.broadcasted_iota(jnp.int32, (rr, rows), 0) < rb
    for g, chosen in enumerate((jnp.where(is_gate, shrink, 0.0), jnp.where(is_gate, 0.0, shrink))):
        for q in range(nreq):
            span = slice(q * blk, (q + 1) * blk)
            s_cols[g, span, :] = chosen[:, span].T.astype(BF16)

    for k in range(nc + 3):
        if k < nc:
            finish(k)
            if k + lead < nc:
                matmul(k + lead)
        if 0 <= k - 1 < nc:
            across(k - 1)
        if 0 <= k - 2 < nc:
            activate(k - 2)
        if 0 <= k - 3 < nc:
            relay(k - 3)

    for k in range(nc):
        cols = pl.ds(k * tn, tn)
        for j in j_peers + [pair]:
            theirs = hid.at[aligned(2 * j + 1 - core, rps), cols]
            remote(theirs, theirs, f_s.at[j, k], f_r.at[j, k], {"sub": mate}).wait_recv()

    for n in range(nd):
        l_d[n].wait()

        def down(c, carry, n=n):
            cols = pl.ds(pl.multiple_of(n * dn + c * dw, 128), dw)
            d_part[:, cols] = jnp.dot(hid[...], d_buf[:, cols], preferred_element_type=F32).astype(BF16)
            return carry

        lax.fori_loop(0, dn // dw, down, 0)
        cols = pl.ds(n * dn, dn)
        for i, p in enumerate(t_peers):
            send(
                d_part.at[aligned(p, rpt), cols],
                d_recv.at[t, :, cols],
                d_s.at[i, n],
                d_r.at[t, n],
                {"tensor": p},
            )

    for n in range(nd):
        cols = pl.ds(n * dn, dn)
        total = d_part[aligned(t, rpt), cols].astype(F32)
        for p in t_peers:
            remote(
                d_part.at[aligned(p, rpt), cols],
                d_recv.at[p, :, cols],
                d_s.at[0, n],
                d_r.at[p, n],
                {"tensor": p},
            ).wait_recv()
            total += d_recv[p, :, cols].astype(F32)
        out_ref[:, cols] = (x_buf[aligned(t, rpt), cols].astype(F32) + total).astype(BF16)

    for copy in sent:
        copy.wait_send()


def shards(mesh, tokens, ids, slots, gate_w, up_w, down_w, imaps, omaps):
    nt, ns = mesh.shape["tensor"], mesh.shape["sub"]
    kept, fcols, rank2 = imaps.shape
    rb = omaps.shape[2]
    rr = 2 * rb
    nreq = ids.shape[0]
    rpt = tokens.shape[0]
    rows = rpt * nt
    hcols, dcols = gate_w.shape[1], down_w.shape[1]
    rps, npair = rows // ns, ns // 2
    tn = tile_of(hcols, (512, 896, 384, 256, 128))
    tw = tile_of(tn, (256, 128))
    dn = tile_of(dcols, (512, 256, 128))
    dw = tile_of(dn, (256, 128))
    nc, nd = hcols // tn, dcols // dn
    lead = min(2, nc)
    cfg = dict(
        nt=nt, ns=ns, req=nreq, kept=kept, rb=rb, rank=rank2 // 2, rows=rows, hcols=hcols, dcols=dcols,
        tn=tn, tw=tw, dn=dn, dw=dw, lead=lead,
    )
    omaps = omaps.reshape(kept, rr, omaps.shape[3])
    dma = pltpu.SemaphoreType.DMA
    scratch = [
        pltpu.VMEM((rows, fcols), BF16),
        pltpu.VMEM((2, fcols, hcols), BF16),
        pltpu.VMEM((hcols, dcols), BF16),
        pltpu.VMEM(imaps.shape, BF16),
        pltpu.VMEM(omaps.shape, BF16),
        pltpu.VMEM((nt, nreq * rr, hcols), BF16),
        pltpu.VMEM((nt, nreq * rr, hcols), BF16),
        pltpu.VMEM((ns, rr, rows), F32),
        pltpu.VMEM((ns, rr, rows), F32),
        pltpu.VMEM((rr, rows), BF16),
        pltpu.VMEM((nt, rr, rows), BF16),
        pltpu.VMEM((2, rows, rr), BF16),
        pltpu.VMEM((lead, 2, rows, tn), F32),
        pltpu.VMEM((2, rows, hcols), BF16),
        pltpu.VMEM((npair, 2, rps, hcols), BF16),
        pltpu.VMEM((npair, 2, rps, hcols), BF16),
        pltpu.VMEM((npair, 2, rps, hcols), BF16),
        pltpu.VMEM((rows, hcols), BF16),
        pltpu.VMEM((rows, dcols), BF16),
        pltpu.VMEM((nt, rpt, dcols), BF16),
        dma((3,)),
        dma((2, nc)),
        dma((nd,)),
        dma((nt,)), dma((nt,)),
        dma((nt, nc)), dma((nt, nc)),
        dma((ns,)), dma((ns,)),
        dma((nt,)), dma((nt,)),
        dma((npair, nc)), dma((npair, nc)),
        dma((npair, nc)), dma((npair, nc)),
        dma((npair, nc)), dma((npair, nc)),
        dma((npair, nc)), dma((npair, nc)),
        dma((nt, nd)), dma((nt, nd)),
    ]
    any_space = pl.BlockSpec(memory_space=pl.ANY)
    smem = pl.BlockSpec(memory_space=pltpu.SMEM)
    weight_bytes = 2 * (2 * fcols * hcols + hcols * dcols)
    return pl.pallas_call(
        functools.partial(block_kernel, cfg),
        out_shape=jax.ShapeDtypeStruct((rpt, dcols), BF16),
        in_specs=[smem, smem] + [any_space] * 6,
        out_specs=pl.BlockSpec(memory_space=pltpu.VMEM),
        scratch_shapes=scratch,
        compiler_params=pltpu.CompilerParams(
            collective_id=0, has_side_effects=True, vmem_limit_bytes=60 * 1024 * 1024
        ),
        cost_estimate=pl.CostEstimate(
            flops=rows * weight_bytes, bytes_accessed=weight_bytes, transcendentals=rps * hcols
        ),
    )(ids, slots, tokens, gate_w, up_w, down_w, imaps, omaps)


def solution(mesh):
    in_specs = (
        P(("groups", "tensor"), "sub"),
        P("groups"),
        P("groups"),
        P("sub", "tensor"),
        P("sub", "tensor"),
        P("tensor", "sub"),
        P(("groups", "tensor"), "sub", None),
        P(("groups", "tensor"), None, "sub", None),
    )
    out_specs = P(("groups", "tensor"), "sub")
    return jax.shard_map(
        functools.partial(shards, mesh), mesh=mesh, in_specs=in_specs, out_specs=out_specs, check_vma=False
    )
```

time: 279 us -> 82.5 us (0.30); the launches traced: 275 us -> 82.4 us
  blocking collectives: 96.1 us -> 0 us
  Pallas kernels: 0 us -> 80.1 us
  waiting for transfers between devices: 62.4 us -> 0 us
  local copies, waits for them, and re-layouts: 47.9 us -> 1.57 us
  matrix products: 32.6 us -> 0 us
  between operations: 15.7 us -> 0.66 us
  other arithmetic: 15 us -> 0 us
  starting transfers between devices: 5.51 us -> 0 us
    pallas_call x0 -> x1, Pallas kernels: none -> 80.1 us  [shards(): pl.pallas_call(functools.partial(block_kernel, cfg), out_shape=jax.ShapeD...]
    psum x1 -> x0, blocking collectives: 56.5 us -> none  [shards(): lax.psum(reduced_piece.reshape(overall_row_count, 2 * combined_rank), ('t...]
    unnamed x5 -> x0, waiting for transfers between devices: 42.5 us -> none
    all_gather x2 -> x0, blocking collectives: 39.6 us -> none  [the longest x1 30.2 us: shards(): collected_rows = lax.all_gather(tokens, 'tensor', axis=0, tiled=True)]
    dot_general x7 -> x0, matrix products: 32.6 us -> none  [the longest x1 8.46 us: shards(): jnp.dot(hidden, down_weight, preferred_element_type=jnp.float32)]
    unnamed x15 -> x1, local copies, waits for them, and re-layouts: 29.9 us -> 1.57 us
    reduce_scatter x1 -> x0, waiting for transfers between devices: 19.9 us -> none  [shards(): lax.psum_scatter(jnp.dot(hidden, down_weight, preferred_element_type=jnp....]
    dot_general x1 -> x0, local copies, waits for them, and re-layouts: 18 us -> none  [shards(): jnp.einsum('np,pmls->nmls', local_selection, adapter_output_maps, preferr...]
  transfers between devices with their start and end apart: 4 -> 0, of which waited for: 3 -> 0; matrix products, arithmetic and copies ran while one was open for 5% -> 0% of each run, Pallas kernels for 0% -> 0%
where the time goes in v1:
time: 82.5 us; the launch traced here: 82.4 us
  Pallas kernels  80.1 us (97%)
  local copies, waits for them, and re-layouts  1.57 us (2%)
    pallas_call x1, Pallas kernels, shards(): pl.pallas_call(functools.partial(block_kernel, cfg), out_shape=jax.ShapeD...  80.1 us

profile of v1, /device:TPU:1, one launch (start us, length us, event | category | flops | bytes accessed | tf_op | source)
XLA Modules:
  0.0 82.4 jit_solution(1709818255825399533)
XLA Ops:
  0.7 80.1 %shard_map.82 = bf16[32,2048]{1,0:T(8,128)(2,1)} custom-call(s32[1]{0:T(128)S(6)} %copy.10.ids_ref, s32[12]{0:T(128)} %slots_ref.1, bf16[32,2048]{1,0:T(8,128)(2,1)} %tok_hbm.1, bf16[2048,3584]{1,0:T(8,128)(2,1)} %gate_hbm.1, bf16[2048,3584]{1,0:T(8,128)(2,1)} %up_hbm.1, bf16[3584,2048]{1,0:T(8,128)(2,1)} %down_hbm.1, bf16[3,2048,128]{2,1,0:T(8,128)(2,1)} %imap_hbm.1, ...), custom_call_target="tpu_custom_call" | custom-call | flops 5637144576 | bytes 44040192 | tf_op jit(solution)/shard_map/pallas_call | solution.py:406
  80.8 1.6 %copy.11 = bf16[32,2048]{1,0:T(8,128)(2,1)} copy(bf16[32,2048]{1,0:T(8,128)(2,1)} %shard_map.82) | data formatting | bytes 262144

commit v2 on v1

--- a/solution.py
+++ b/solution.py
@@ -138,17 +138,25 @@
         for c in range(nt):
             theirs = omap[local[q], :, c * hcols : (c + 1) * hcols]
             b_send[c, q * rr : (q + 1) * rr, :] = (theirs.astype(F32) * mine[q]).astype(BF16)
-    for k in range(nc):
-        cols = pl.ds(k * tn, tn)
-        for i, p in enumerate(t_peers):
-            send(
-                b_send.at[p, :, cols],
-                b_recv.at[t, :, cols],
-                b_s.at[i, k],
-                b_r.at[t, k],
-                {"tensor": p},
-            )
-
+    map_copies = []
+
+    def send_maps():
+        k = len(map_copies)
+        if k == nc:
+            return
+        if k > 0:
+            for copy in map_copies[-1]:
+                copy.wait_send()
+        cols = pl.ds(k * tn, tn)
+        copies = [
+            remote(b_send.at[p, :, cols], b_recv.at[t, :, cols], b_s.at[i, k], b_r.at[t, k], {"tensor": p})
+            for i, p in enumerate(t_peers)
+        ]
+        for copy in copies:
+            copy.start()
+        map_copies.append(copies)
+
+    send_maps()
     l_imap.wait()
     l_tok.wait()
     for p in t_peers:
@@ -164,6 +172,7 @@
     for i, p in enumerate(s_peers):
         send(sh1_send.at[p], sh1_recv.at[s], sh1_s.at[i], sh1_r.at[s], {"sub": p})
 
+    send_maps()
     l_d = []
     for n in range(nd):
         cols = pl.ds(n * dn, dn)
@@ -189,6 +198,7 @@
         lax.fori_loop(0, 2 * per, body, 0)
 
     def finish(k):
+        send_maps()
         cols = pl.ds(k * tn, tn)
         for p in t_peers:
             remote(
@@ -276,6 +286,7 @@
     for i, p in enumerate(t_peers):
         send(sh2_send, sh2_recv.at[t], sh2_s.at[i], sh2_r.at[t], {"tensor": p})
 
+    send_maps()
     for k in range(1, lead):
         matmul(k)
 
@@ -340,7 +351,7 @@
             total += d_recv[p, :, cols].astype(F32)
         out_ref[:, cols] = (x_buf[aligned(t, rpt), cols].astype(F32) + total).astype(BF16)
 
-    for copy in sent:
+    for copy in map_copies[-1] + sent:
         copy.wait_send()
 
 
@@ -354,8 +365,8 @@
     rows = rpt * nt
     hcols, dcols = gate_w.shape[1], down_w.shape[1]
     rps, npair = rows // ns, ns // 2
-    tn = tile_of(hcols, (512, 896, 384, 256, 128))
-    tw = tile_of(tn, (256, 128))
+    tn = tile_of(hcols, (896, 512, 384, 256, 128))
+    tw = tile_of(tn, (896, 256, 128))
     dn = tile_of(dcols, (512, 256, 128))
     dw = tile_of(dn, (256, 128))
     nc, nd = hcols // tn, dcols // dn

time: 82.5 us -> 72.7 us (0.88)
  Pallas kernels: 80.1 us -> 69.8 us
    pallas_call x1, Pallas kernels: 80.1 us -> 69.8 us  [shards(): pl.pallas_call(functools.partial(block_kernel, cfg), out_shape=jax.ShapeD...]
where the time goes in v2:
time: 72.7 us; the launch traced here: 72 us
  Pallas kernels  69.8 us (96%)
  local copies, waits for them, and re-layouts  1.57 us (2%)
    pallas_call x1, Pallas kernels, shards(): pl.pallas_call(functools.partial(block_kernel, cfg), out_shape=jax.ShapeD...  69.8 us
    unnamed x1, local copies, waits for them, and re-layouts  1.57 us

profile of v2, /device:TPU:1, one launch (start us, length us, event | category | flops | bytes accessed | tf_op | source)
XLA Modules:
  0.0 72.0 jit_solution(8477999916998020478)
XLA Ops:
  0.7 69.8 %shard_map.82 = bf16[32,2048]{1,0:T(8,128)(2,1)} custom-call(s32[1]{0:T(128)S(6)} %copy.10.ids_ref, s32[12]{0:T(128)} %slots_ref.1, bf16[32,2048]{1,0:T(8,128)(2,1)} %tok_hbm.1, bf16[2048,3584]{1,0:T(8,128)(2,1)} %gate_hbm.1, bf16[2048,3584]{1,0:T(8,128)(2,1)} %up_hbm.1, bf16[3584,2048]{1,0:T(8,128)(2,1)} %down_hbm.1, bf16[3,2048,128]{2,1,0:T(8,128)(2,1)} %imap_hbm.1, ...), custom_call_target="tpu_custom_call" | custom-call | flops 5637144576 | bytes 44040192 | tf_op jit(solution)/shard_map/pallas_call | solution.py:417
  70.5 1.6 %copy.11 = bf16[32,2048]{1,0:T(8,128)(2,1)} copy(bf16[32,2048]{1,0:T(8,128)(2,1)} %shard_map.82) | data formatting | bytes 262144

commit v3 on v2

--- a/solution.py
+++ b/solution.py
@@ -156,11 +156,12 @@
             copy.start()
         map_copies.append(copies)
 
-    send_maps()
     l_imap.wait()
     l_tok.wait()
     for p in t_peers:
         remote(tok_hbm, x_buf.at[aligned(p, rpt), :], tok_s.at[0], tok_r.at[p], {"tensor": p}).wait_recv()
+
+    send_maps()
 
     for q in range(nreq):
         span = slice(q * blk, (q + 1) * blk)
@@ -172,7 +173,6 @@
     for i, p in enumerate(s_peers):
         send(sh1_send.at[p], sh1_recv.at[s], sh1_s.at[i], sh1_r.at[s], {"sub": p})
 
-    send_maps()
     l_d = []
     for n in range(nd):
         cols = pl.ds(n * dn, dn)

time: 72.7 us -> 71.2 us (0.979)
  Pallas kernels: 69.8 us -> 68.8 us
    pallas_call x1, Pallas kernels: 69.8 us -> 68.8 us  [shards(): pl.pallas_call(functools.partial(block_kernel, cfg), out_shape=jax.ShapeD...]
where the time goes in v3:
time: 71.2 us; the launch traced here: 71 us
  Pallas kernels  68.8 us (97%)
  local copies, waits for them, and re-layouts  1.57 us (2%)
    pallas_call x1, Pallas kernels, shards(): pl.pallas_call(functools.partial(block_kernel, cfg), out_shape=jax.ShapeD...  68.8 us
    unnamed x1, local copies, waits for them, and re-layouts  1.57 us

profile of v3, /device:TPU:1, one launch (start us, length us, event | category | flops | bytes accessed | tf_op | source)
XLA Modules:
  0.0 71.0 jit_solution(17837888666666477171)
XLA Ops:
  0.7 68.8 %shard_map.82 = bf16[32,2048]{1,0:T(8,128)(2,1)} custom-call(s32[1]{0:T(128)S(6)} %copy.10.ids_ref, s32[12]{0:T(128)} %slots_ref.1, bf16[32,2048]{1,0:T(8,128)(2,1)} %tok_hbm.1, bf16[2048,3584]{1,0:T(8,128)(2,1)} %gate_hbm.1, bf16[2048,3584]{1,0:T(8,128)(2,1)} %up_hbm.1, bf16[3584,2048]{1,0:T(8,128)(2,1)} %down_hbm.1, bf16[3,2048,128]{2,1,0:T(8,128)(2,1)} %imap_hbm.1, ...), custom_call_target="tpu_custom_call" | custom-call | flops 5637144576 | bytes 44040192 | tf_op jit(solution)/shard_map/pallas_call | solution.py:417
  69.4 1.6 %copy.11 = bf16[32,2048]{1,0:T(8,128)(2,1)} copy(bf16[32,2048]{1,0:T(8,128)(2,1)} %shard_map.82) | data formatting | bytes 262144
